TPU v7x, 512 devices: a whole 4x8x8 slice. The times are simulated.
512 devices in a mesh: reg: 16 (over z, core), prod: 32 (over x, y).
Axes of the slice: x: 4, y: 8, z: 8, core: 2. Of those that a mesh axis runs over, the one named last changes fastest.
Arguments:
- panel_factor: float32 [131072, 2048], P('reg', 'prod'), may hold values from -0.125 to 0.125
- block_inverse: float32 [2048, 2048], P('prod', 'reg'), may hold values from -1 to 2.5
- panel_rhs: float32 [2048, 1024], P('reg'), may hold values from -6 to 6
- trailing_rhs: float32 [131072, 1024], P(('reg', 'prod')), may hold values from -6 to 6
Outputs:
- solved: float32 [2048, 1024], P('prod', 'reg')
- updated: float32 [131072, 1024], P(('reg', 'prod'))
All inputs are finite; a program needn't handle non-finite values.
Results may differ from a plain program's by a relative error of at most 0.000075.
Values sent between devices are 32-bit elements; how exact they have to be, the bound alone decides.
A program may use at most 64 MiB of HBM per device.

v0:
```python
import jax
import jax.numpy as jnp
from jax import lax
from jax.sharding import PartitionSpec as P


def local(panel_factor, block_inverse, panel_rhs, trailing_rhs):
    partial_product = jnp.dot(
        block_inverse,
        panel_rhs,
        precision=lax.Precision.HIGHEST,
        preferred_element_type=jnp.float32,
    )
    factor_rows = lax.all_to_all(panel_factor, "prod", split_axis=0, concat_axis=1, tiled=True)
    solved_rows = lax.psum(partial_product, "reg")
    updated = trailing_rhs - jnp.dot(
        factor_rows,
        lax.all_gather(solved_rows, "prod", axis=0, tiled=True),
        precision=lax.Precision.HIGHEST,
        preferred_element_type=jnp.float32,
    )
    share_width = solved_rows.shape[1] // lax.axis_size("reg")
    solved = lax.dynamic_slice_in_dim(
        solved_rows, lax.axis_index("reg") * share_width, share_width, 1
    )
    return (solved, updated)


def solution(mesh):
    in_specs = (P("reg", "prod"), P("prod", "reg"), P("reg", None), P(("reg", "prod"), None))
    out_specs = (P("prod", "reg"), P(("reg", "prod"), None))
    return jax.shard_map(local, mesh=mesh, in_specs=in_specs, out_specs=out_specs, check_vma=False)
```

profile of v0, /device:TPU:1, one launch (start us, length us, event | category | flops | bytes accessed | tf_op | source)
XLA Modules:
  0.0 280.5 jit_solution(15664980325464303684)
XLA Ops:
  7.2 0.0 copy-start
  7.2 0.0 all-reduce.2.cloned.1.call-start
  7.2 1.0 copy-done
  8.2 1.9 fusion.1
  10.1 0.0 all-reduce.2.cloned.1.call-update
  10.1 0.0 all-gather.2.cloned.1.call-start
  10.2 120.9 %all-reduce.2.cloned.1.call-done = f32[64,1024]{1,0:T(8,128)} async-done(((f32[64,1024]{1,0:T(8,128)}), f32[64,1024]{1,0:T(8,128)}) %all-reduce.2.cloned.1.call-update) | async-done | bytes 262160 | tf_op jit(solution)/shard_map/psum | solution.py:15
  131.1 0.0 all-gather.2.cloned.1.call-update
  131.1 3.2 %copy.18 = f32[8,32,8,256]{3,2,0,1:T(8,128)} copy(f32[8,32,8,256]{3,2,1,0:T(8,128)} %bitcast.17) | data formatting | bytes 4194304 | tf_op jit(solution)/shard_map/all_to_all | solution.py:14
  134.3 9.3 %all-to-all-start = ((f32[32,256,64]{1,2,0:T(8,128)}), f32[32,256,64]{1,2,0:T(8,128)S(1)}, u32[]{:S(2)}, u32[]{:S(2)}) async-start(f32[32,256,64]{1,2,0:T(8,128)} %bitcast.16), calls=%async_computation | async-start | bytes 4194304 | tf_op jit(solution)/shard_map/all_to_all | solution.py:14
  143.6 2.5 copy.14
  146.1 1.4 constant_dynamic-slice_fusion
  147.6 55.0 %all-to-all-done = f32[32,256,64]{1,2,0:T(8,128)S(1)} async-done(((f32[32,256,64]{1,2,0:T(8,128)}), f32[32,256,64]{1,2,0:T(8,128)S(1)}, u32[]{:S(2)}, u32[]{:S(2)}) %all-to-all-start) | async-done | bytes 2097184 | tf_op jit(solution)/shard_map/all_to_all | solution.py:14
  202.6 52.1 %all-gather.2.cloned.1.call-done = f32[2048,1024]{1,0:T(8,128)} async-done(((f32[64,1024]{1,0:T(8,128)}), f32[2048,1024]{1,0:T(8,128)}) %all-gather.2.cloned.1.call-update) | async-done | bytes 8388624 | tf_op jit(solution)/shard_map/all_gather | solution.py:18
  254.7 16.5 %fusion = f32[256,1024]{0,1:T(8,128)} fusion(f32[256,1024]{0,1:T(8,128)} %copy.14, f32[2048,1024]{1,0:T(8,128)} %all-gather.2.cloned.1.call-done, f32[256,2048]{0,1:T(8,128)S(1)} %bitcast.15), kind=kOutput, calls=%fused_computation.2 | convolution fusion | flops 6442713088 | bytes 12582912 | tf_op jit(solution)/shard_map/dot_general | solution.py:16
  271.2 2.5 copy.15
Async XLA Ops:
  7.2 1.0 copy-start
  7.2 123.9 %all-reduce.2.cloned.1.call-start = ((), (), s32[]{:S(2)}) async-start(), calls=%async_computation.1 | async-start | bytes 524288 | tf_op jit(solution)/shard_map/psum | solution.py:15
  10.1 244.5 %all-gather.2.cloned.1.call-start = ((), (), s32[]{:S(2)}) async-start(), calls=%async_computation.2 | async-start | bytes 8650752 | tf_op jit(solution)/shard_map/all_gather | solution.py:18
  134.3 68.3 %all-to-all-start = ((f32[32,256,64]{1,2,0:T(8,128)}), f32[32,256,64]{1,2,0:T(8,128)S(1)}, u32[]{:S(2)}, u32[]{:S(2)}) async-start(f32[32,256,64]{1,2,0:T(8,128)} %bitcast.16), calls=%async_computation | async-start | bytes 4194304 | tf_op jit(solution)/shard_map/all_to_all | solution.py:14
Sparse Core Ops, SparseCore 0:
  10.9 120.1 all-reduce.1
  134.7 119.9 all-gather.1
where the time goes:
time: 281 us
  waiting for transfers between devices  228 us (81%)
  matrix products  18.4 us (7%)
  between operations  14.1 us (5%)
  local copies, waits for them, and re-layouts  10.7 us (4%)
  starting transfers between devices  9.34 us (3%)
    psum x1, waiting for transfers between devices, local(): solved_rows = lax.psum(partial_product, 'reg')  121 us
    all_to_all x1, waiting for transfers between devices, local(): lax.all_to_all(panel_factor, 'prod', split_axis=0, concat_axis=1, tiled=T...  55 us
    all_gather x1, waiting for transfers between devices, local(): lax.all_gather(solved_rows, 'prod', axis=0, tiled=True)  52.1 us
    dot_general x1, matrix products, local(): jnp.dot(factor_rows, lax.all_gather(solved_rows, 'prod', axis=0, tiled=Tr...  16.5 us
    all_to_all x1, starting transfers between devices, local(): lax.all_to_all(panel_factor, 'prod', split_axis=0, concat_axis=1, tiled=T...  9.26 us
    unnamed x4, local copies, waits for them, and re-layouts  6.06 us
  transfers between devices with their start and end apart: 3, of which 3 were waited for; matrix products, arithmetic and copies ran while one was open for 3% of the time, Pallas kernels for 0%

commit v1 on v0

v1 whole, which is shorter than its diff:
```python
import functools

import jax
import jax.numpy as jnp
from jax import lax
from jax.experimental import pallas as pl
from jax.experimental.pallas import tpu as pltpu
from jax.sharding import PartitionSpec as P

MESH = pl.DeviceIdType.MESH
NX, NY, NZ = 4, 8, 8
F32, BF16 = jnp.float32, jnp.bfloat16


def kernel(
    ft_ref, b_ref, p_ref, t_ref, solved_ref, out_ref,
    b_v, p_v, t_v, o_v, sv_v, part, landed, g, fg, a_hi, a_lo, s_hi, s_lo,
    loc_sem, o_sem, rs_s, rs_r, f_s, f_r, y_s, y_r, x_s, x_r, z_s, z_r, c_s, c_r,
):
    reg, prod = lax.axis_index("reg"), lax.axis_index("prod")
    z, c = reg // 2, reg % 2
    x, y = prod // NY, prod % NY
    sibling = z * 2 + 1 - c

    def send(src, dst, s, r, to_reg, to_prod):
        return pltpu.make_async_remote_copy(
            src_ref=src, dst_ref=dst, send_sem=s, recv_sem=r,
            device_id=(to_reg, to_prod), device_id_type=MESH,
        )

    load_b = pltpu.make_async_copy(b_ref, b_v, loc_sem.at[0])
    load_p = pltpu.make_async_copy(p_ref, p_v, loc_sem.at[1])
    load_t = pltpu.make_async_copy(t_ref, t_v, loc_sem.at[2])
    load_f = pltpu.make_async_copy(
        ft_ref.at[:, :, pl.ds(pl.multiple_of(prod * 256, 256), 256)], fg.at[:, prod], loc_sem.at[3]
    )
    load_b.start()
    load_p.start()

    barrier = pltpu.get_barrier_semaphore()
    for d in range(1, 2 * NZ):
        pl.semaphore_signal(barrier, inc=1, device_id=((reg + d) % (2 * NZ), prod), device_id_type=MESH)
    for d in range(1, NX * NY):
        pl.semaphore_signal(barrier, inc=1, device_id=(reg, (prod + d) % (NX * NY)), device_id_type=MESH)

    load_b.wait()
    load_p.wait()
    product = jnp.dot(b_v[...], p_v[...], precision=lax.Precision.HIGHEST, preferred_element_type=F32)
    for i in range(2 * NZ):
        part[i] = product[(i % 2) * 32:(i % 2) * 32 + 32, (i // 2) * 128:(i // 2) * 128 + 128]

    pl.semaphore_wait(barrier, 2 * NZ - 1 + NX * NY - 1)

    sends = []

    def go(copy):
        copy.start()
        sends.append(copy)

    rs = []
    for d in range(1, 2 * NZ):
        to = (reg + d) % (2 * NZ)
        copy = send(part.at[to], landed.at[reg], rs_s.at[d], rs_r.at[d], to, prod)
        go(copy)
        rs.append(copy)

    factor = []
    for dy in (4, 3, 5, 2, 6, 1, 7, 0):
        for dx in (2, 1, 3, 0):
            if dx == 0 and dy == 0:
                continue
            to = ((x + dx) % NX) * NY + (y + dy) % NY
            i = dx * NY + dy
            copy = send(
                ft_ref.at[:, :, pl.ds(pl.multiple_of(to * 256, 256), 256)],
                fg.at[:, prod], f_s.at[i], f_r.at[i], reg, to,
            )
            go(copy)
            factor.append(copy)
    load_f.start()
    load_t.start()

    landed[reg] = part[reg]
    for copy in rs:
        copy.wait_recv()
    g[z, c, prod] = jnp.sum(landed[...], axis=0)

    ys = []
    for dy in (1, 7, 2, 6, 3, 5, 4):
        copy = send(
            g.at[z, c, prod], g.at[z, c, prod], y_s.at[dy], y_r.at[dy], reg, x * NY + (y + dy) % NY
        )
        go(copy)
        ys.append(copy)
    for copy in ys:
        copy.wait_recv()

    def unit(zs, cs, j):
        return g.at[zs, cs, pl.ds(((x + j) % NX) * NY, NY)]

    def relay(zs, slot, j, right, left):
        u = unit(zs, c, j)
        if right is not None:
            go(send(u, u, z_s.at[0, right, j], z_r.at[0, right, j], ((z + 1) % NZ) * 2 + c, prod))
        if left is not None:
            go(send(u, u, z_s.at[1, left, j], z_r.at[1, left, j], ((z + NZ - 1) % NZ) * 2 + c, prod))
        go(send(u, u, c_s.at[slot, j], c_r.at[slot, j], sibling, prod))

    xs = {}
    for dx in (1, 3, 2):
        u = unit(z, c, 0)
        copy = send(u, u, x_s.at[dx], x_r.at[dx], reg, ((x + dx) % NX) * NY + y)
        go(copy)
        xs[(NX - dx) % NX] = copy
    relay(z, 0, 0, 0, 0)
    for j in (1, 3, 2):
        xs[j].wait_recv()
        relay(z, 0, j, 0, 0)

    def arrive(way, hop, j):
        zs = (z + NZ - hop) % NZ if way == 0 else (z + hop) % NZ
        u = unit(zs, c, j)
        send(u, u, z_s.at[way, hop - 1, j], z_r.at[way, hop - 1, j], reg, prod).wait_recv()
        onward = hop < 3 or (hop == 3 and (j < 2) == (way == 0))
        slot = 7 if hop == 4 else hop + 3 * way
        relay(
            zs, slot, j,
            hop if way == 0 and onward else None,
            hop if way == 1 and onward else None,
        )

    def from_sibling(slot, zs):
        for j in range(NX):
            u = unit(zs, 1 - c, j)
            send(u, u, c_s.at[slot, j], c_r.at[slot, j], reg, prod).wait_recv()

    def factor_in():
        load_f.wait()
        for copy in factor:
            copy.wait_recv()
        for cs in range(2):
            for j in range(NX):
                block = fg[cs, j * NY:(j + 1) * NY].reshape(256, 256).T
                hi = block.astype(BF16)
                k = (cs * NX + j) * 256
                a_hi[:, k:k + 256] = hi
                a_lo[:, k:k + 256] = (block - hi.astype(F32)).astype(BF16)

    def multiply(za, zb):
        for half, zs in enumerate((za, zb)):
            block = g[zs].reshape(2048, 128)
            hi = block.astype(BF16)
            s_hi[:, half * 128:half * 128 + 128] = hi
            s_lo[:, half * 128:half * 128 + 128] = (block - hi.astype(F32)).astype(BF16)
        acc = jnp.dot(a_hi[...], s_lo[...], preferred_element_type=F32)
        acc += jnp.dot(a_lo[...], s_hi[...], preferred_element_type=F32)
        acc += jnp.dot(a_hi[...], s_hi[...], preferred_element_type=F32)
        for half, zs in enumerate((za, zb)):
            cols = pl.ds(pl.multiple_of(zs * 128, 128), 128)
            o_v[:, cols] = t_v[:, cols] - acc[:, half * 128:half * 128 + 128]

    for hop in (1, 2, 3):
        for j in (0, 1, 3, 2):
            arrive(0, hop, j)
            arrive(1, hop, j)
    for j in range(NX):
        arrive(0 if j < 2 else 1, 4, j)

    from_sibling(0, z)
    own = jnp.concatenate([g[z, 0, prod], g[z, 1, prod]], axis=0)
    sv_v[...] = jnp.where(c == 0, own[:, :64], own[:, 64:])
    store_s = pltpu.make_async_copy(sv_v, solved_ref, loc_sem.at[4])
    store_s.start()

    load_t.wait()
    factor_in()
    for hop in (1, 2, 3):
        za, zb = (z + NZ - hop) % NZ, (z + hop) % NZ
        from_sibling(hop, za)
        from_sibling(hop + 3, zb)
        multiply(za, zb)
    from_sibling(7, (z + 4) % NZ)
    multiply(z, (z + 4) % NZ)
    store = pltpu.make_async_copy(o_v, out_ref, o_sem.at[0])
    store.start()
    for copy in sends:
        copy.wait_send()
    store.wait()
    store_s.wait()


def local(panel_factor, block_inverse, panel_rhs, trailing_rhs):
    ft = panel_factor.T.reshape(2, 32, 8192)
    dma = pltpu.SemaphoreType.DMA
    any_spec = pl.BlockSpec(memory_space=pl.ANY)
    return pl.pallas_call(
        kernel,
        out_shape=(
            jax.ShapeDtypeStruct((64, 64), F32),
            jax.ShapeDtypeStruct((256, 1024), F32),
        ),
        in_specs=[any_spec] * 4,
        out_specs=(any_spec, any_spec),
        scratch_shapes=[
            pltpu.VMEM((64, 128), F32),
            pltpu.VMEM((128, 1024), F32),
            pltpu.VMEM((256, 1024), F32),
            pltpu.VMEM((256, 1024), F32),
            pltpu.VMEM((64, 64), F32),
            pltpu.VMEM((16, 32, 128), F32),
            pltpu.VMEM((16, 32, 128), F32),
            pltpu.VMEM((8, 2, 32, 32, 128), F32),
            pltpu.VMEM((2, 32, 32, 256), F32),
            pltpu.VMEM((256, 2048), BF16),
            pltpu.VMEM((256, 2048), BF16),
            pltpu.VMEM((2048, 256), BF16),
            pltpu.VMEM((2048, 256), BF16),
            dma((5,)),
            dma((1,)),
            dma((16,)),
            dma((16,)),
            dma((32,)),
            dma((32,)),
            dma((8,)),
            dma((8,)),
            dma((4,)),
            dma((4,)),
            dma((2, 4, 4)),
            dma((2, 4, 4)),
            dma((8, 4)),
            dma((8, 4)),
        ],
        compiler_params=pltpu.CompilerParams(
            collective_id=0, has_side_effects=True, vmem_limit_bytes=40 * 1024 * 1024
        ),
        name="panel_step",
    )(ft, block_inverse, panel_rhs, trailing_rhs)


def solution(mesh):
    in_specs = (P("reg", "prod"), P("prod", "reg"), P("reg", None), P(("reg", "prod"), None))
    out_specs = (P("prod", "reg"), P(("reg", "prod"), None))
    return jax.shard_map(local, mesh=mesh, in_specs=in_specs, out_specs=out_specs, check_vma=False)
```

time: 281 us -> 128 us (0.46)
  waiting for transfers between devices: 228 us -> 0 us
  Pallas kernels: 0 us -> 119 us
  matrix products: 18.4 us -> 0 us
  between operations: 14.1 us -> 0.65 us
  starting transfers between devices: 9.34 us -> 0 us
  local copies, waits for them, and re-layouts: 10.7 us -> 6.19 us
    psum x1 -> x0, waiting for transfers between devices: 121 us -> none  [local(): solved_rows = lax.psum(partial_product, 'reg')]
    pallas_call x0 -> x1, Pallas kernels: none -> 119 us  [local(): pl.pallas_call(kernel, out_shape=(jax.ShapeDtypeStruct((64, 64), F32), ja...]
    all_to_all x1 -> x0, waiting for transfers between devices: 55 us -> none  [local(): lax.all_to_all(panel_factor, 'prod', split_axis=0, concat_axis=1, tiled=T...]
    all_gather x1 -> x0, waiting for transfers between devices: 52.1 us -> none  [local(): lax.all_gather(solved_rows, 'prod', axis=0, tiled=True)]
    dot_general x2 -> x0, matrix products: 18.4 us -> none  [the longest x1 16.5 us: local(): jnp.dot(factor_rows, lax.all_gather(solved_rows, 'prod', axis=0, tiled=Tr...]
    all_to_all x1 -> x0, starting transfers between devices: 9.26 us -> none  [local(): lax.all_to_all(panel_factor, 'prod', split_axis=0, concat_axis=1, tiled=T...]
    all_to_all x1 -> x0, local copies, waits for them, and re-layouts: 3.23 us -> none  [local(): lax.all_to_all(panel_factor, 'prod', split_axis=0, concat_axis=1, tiled=T...]
    unnamed x4 -> x10, local copies, waits for them, and re-layouts: 6.06 us -> 6.19 us
  transfers between devices with their start and end apart: 3 -> 0, of which waited for: 3 -> 0; matrix products, arithmetic and copies ran while one was open for 3% -> 0% of each run, Pallas kernels for 0% -> 0%
where the time goes in v1:
time: 128 us; the launch traced here: 125 us
  Pallas kernels  119 us (93%)
  local copies, waits for them, and re-layouts  6.19 us (5%)
    pallas_call x1, Pallas kernels, local(): pl.pallas_call(kernel, out_shape=(jax.ShapeDtypeStruct((64, 64), F32), ja...  119 us
    unnamed x10, local copies, waits for them, and re-layouts  6.19 us

profile of v1, /device:TPU:1, one launch (start us, length us, event | category | flops | bytes accessed | tf_op | source)
XLA Modules:
  0.0 125.5 jit_solution(15051569422233070226)
XLA Ops:
  0.6 0.0 copy-start
  0.6 1.6 %copy-done = f32[8192,64]{0,1:T(8,128)S(1)} copy-done((f32[8192,64]{0,1:T(8,128)S(1)}, f32[8192,64]{0,1:T(8,128)}, u32[]{:S(2)}) %copy-start) | copy-done | bytes 2097176
  2.2 0.0 copy-start.1
  2.2 1.2 copy-done.1
  3.4 0.0 copy-start.2
  3.5 1.0 copy-done.2
  4.5 0.0 copy-start.3
  4.5 0.8 copy-done.3
  5.2 118.6 %panel_step.1 = (f32[64,64]{1,0:T(8,128)S(1)}, f32[256,1024]{1,0:T(8,128)S(1)}) custom-call(f32[2,32,8192]{2,1,0:T(8,128)S(1)} %bitcast.3, f32[64,128]{1,0:T(8,128)S(1)} %copy-done.3, f32[128,1024]{1,0:T(8,128)S(1)} %copy-done.2, f32[256,1024]{1,0:T(8,128)S(1)} %copy-done.1), custom_call_target="tpu_custom_call" | custom-call | tf_op jit(solution)/shard_map/panel_step/pallas_call | solution.py:196
  123.9 0.6 copy.8
  124.5 1.0 copy.9
Async XLA Ops:
  0.6 1.6 %copy-start = (f32[8192,64]{0,1:T(8,128)S(1)}, f32[8192,64]{0,1:T(8,128)}, u32[]{:S(2)}) copy-start(f32[8192,64]{0,1:T(8,128)} %param.4) | copy-start | bytes 6291460
  2.2 1.2 copy-start.1
  3.4 1.0 copy-start.2
  4.5 0.8 copy-start.3

commit v2 on v1

v2 whole, which is shorter than its diff:
```python
import functools

import jax
import jax.numpy as jnp
from jax import lax
from jax.experimental import pallas as pl
from jax.experimental.pallas import tpu as pltpu
from jax.sharding import PartitionSpec as P

MESH = pl.DeviceIdType.MESH
NX, NY, NZ = 4, 8, 8
F32, BF16 = jnp.float32, jnp.bfloat16


def split(block):
    hi = block.astype(BF16)
    return hi, (block - hi.astype(F32)).astype(BF16)


def dot3(a_hi, a_lo, b_hi, b_lo):
    acc = jnp.dot(a_hi, b_lo, preferred_element_type=F32)
    acc += jnp.dot(a_lo, b_hi, preferred_element_type=F32)
    return acc + jnp.dot(a_hi, b_hi, preferred_element_type=F32)


FIRST, SECOND, EACH = 4, 0, 1


def kernel(
    ft_ref, b_ref, p_ref, t_ref, solved_ref, out_ref,
    b_v, p_v, acc, sv_v, part, landed, g, fg, a_hi, a_lo, s_hi, s_lo,
    loc_sem, t_sem, o_sem, rs_s, rs_r, f_s, f_r, y_s, y_r, x_s, x_r, z_s, z_r, c_s, c_r,
):
    reg, prod = lax.axis_index("reg"), lax.axis_index("prod")
    z, c = reg // 2, reg % 2
    x, y = prod // NY, prod % NY
    sibling = z * 2 + 1 - c

    def send(src, dst, s, r, to_reg, to_prod):
        return pltpu.make_async_remote_copy(
            src_ref=src, dst_ref=dst, send_sem=s, recv_sem=r,
            device_id=(to_reg, to_prod), device_id_type=MESH,
        )

    load_b = pltpu.make_async_copy(b_ref, b_v, loc_sem.at[0])
    load_p = pltpu.make_async_copy(p_ref, p_v, loc_sem.at[1])
    load_f = pltpu.make_async_copy(
        ft_ref.at[:, :, pl.ds(pl.multiple_of(prod * 256, 256), 256)], fg.at[:, prod], loc_sem.at[2]
    )
    load_b.start()
    load_p.start()

    barrier = pltpu.get_barrier_semaphore()
    for d in range(1, 2 * NZ):
        pl.semaphore_signal(barrier, inc=1, device_id=((reg + d) % (2 * NZ), prod), device_id_type=MESH)
    for d in range(1, NX * NY):
        pl.semaphore_signal(barrier, inc=1, device_id=(reg, (prod + d) % (NX * NY)), device_id_type=MESH)

    def chunk_of(slot):
        if slot < 4:
            return (z + NZ - slot) % NZ
        return (z + slot - 3) % NZ

    def columns(slot):
        return pl.ds(pl.multiple_of(chunk_of(slot) * 128, 128), 128)

    load_b.wait()
    load_p.wait()
    product = dot3(*split(b_v[...]), *split(p_v[...]))
    for i in range(2 * NZ):
        part[i] = product[(i % 2) * 32:(i % 2) * 32 + 32, (i // 2) * 128:(i // 2) * 128 + 128]

    pl.semaphore_wait(barrier, 2 * NZ - 1 + NX * NY - 1)

    sends = []

    def go(copy):
        copy.start()
        sends.append(copy)

    rs = []
    for d in range(1, 2 * NZ):
        to = (reg + d) % (2 * NZ)
        copy = send(part.at[to], landed.at[reg], rs_s.at[d], rs_r.at[d], to, prod)
        go(copy)
        rs.append(copy)

    factor, queue = {}, []
    for dx in (0, 1, 3, 2):
        for dy in (4, 3, 5, 2, 6, 1, 7, 0):
            if dx == 0 and dy == 0:
                continue
            to = ((x + dx) % NX) * NY + (y + dy) % NY
            i = dx * NY + dy
            copy = send(
                ft_ref.at[:, :, pl.ds(pl.multiple_of(to * 256, 256), 256)],
                fg.at[:, prod], f_s.at[i], f_r.at[i], reg, to,
            )
            queue.append(copy)
            factor.setdefault((NX - dx) % NX, []).append(copy)

    def pump(count):
        for _ in range(min(count, len(queue))):
            go(queue.pop(0))

    pump(FIRST)
    load_f.start()
    loads = []
    for slot in range(NZ):
        loads.append(pltpu.make_async_copy(t_ref.at[:, columns(slot)], acc.at[slot], t_sem.at[slot]))
        loads[-1].start()

    landed[reg] = part[reg]
    for copy in rs:
        copy.wait_recv()
    g[z, c, prod] = jnp.sum(landed[...], axis=0)

    ys = []
    for dy in (1, 7, 2, 6, 3, 5, 4):
        copy = send(
            g.at[z, c, prod], g.at[z, c, prod], y_s.at[dy], y_r.at[dy], reg, x * NY + (y + dy) % NY
        )
        go(copy)
        ys.append(copy)
    pump(SECOND)
    for copy in ys:
        copy.wait_recv()

    def unit(zs, cs, j):
        return g.at[zs, cs, pl.ds(((x + j) % NX) * NY, NY)]

    def relay(slot, j, right, left):
        u = unit(chunk_of(slot), c, j)
        if right is not None:
            go(send(u, u, z_s.at[0, right, j], z_r.at[0, right, j], ((z + 1) % NZ) * 2 + c, prod))
        if left is not None:
            go(send(u, u, z_s.at[1, left, j], z_r.at[1, left, j], ((z + NZ - 1) % NZ) * 2 + c, prod))
        go(send(u, u, c_s.at[slot, j], c_r.at[slot, j], sibling, prod))
        pump(EACH)

    xs = {}
    for dx in (1, 3, 2):
        u = unit(z, c, 0)
        copy = send(u, u, x_s.at[dx], x_r.at[dx], reg, ((x + dx) % NX) * NY + y)
        go(copy)
        xs[(NX - dx) % NX] = copy
    relay(0, 0, 0, 0)
    for j in (1, 3, 2):
        xs[j].wait_recv()
        relay(0, j, 0, 0)

    def arrive(way, hop, j):
        slot = 7 if hop == 4 else hop + 3 * way
        u = unit(chunk_of(slot), c, j)
        send(u, u, z_s.at[way, hop - 1, j], z_r.at[way, hop - 1, j], reg, prod).wait_recv()
        onward = hop < 3 or (hop == 3 and (j < 2) == (way == 0))
        relay(
            slot, j,
            hop if way == 0 and onward else None,
            hop if way == 1 and onward else None,
        )

    pairs = ((1, 4), (2, 5), (3, 6), (0, 7))

    def chunk_in(pair, half):
        slot = pairs[pair][half]
        for j in range(NX):
            u = unit(chunk_of(slot), 1 - c, j)
            send(u, u, c_s.at[slot, j], c_r.at[slot, j], reg, prod).wait_recv()
            for cs in range(2):
                hi, lo = split(unit(chunk_of(slot), cs, j)[...].reshape(256, 128))
                s_hi[pair, j, cs * 256:cs * 256 + 256, half * 128:half * 128 + 128] = hi
                s_lo[pair, j, cs * 256:cs * 256 + 256, half * 128:half * 128 + 128] = lo

    def factor_in(j):
        if j == 0:
            load_f.wait()
        for copy in factor[j]:
            copy.wait_recv()
        for cs in range(2):
            block = fg[cs, pl.ds(((x + j) % NX) * NY, NY)].reshape(256, 256).T
            hi, lo = split(block)
            a_hi[j, :, cs * 256:cs * 256 + 256] = hi
            a_lo[j, :, cs * 256:cs * 256 + 256] = lo

    def multiply(j, pair):
        term = dot3(a_hi[j], a_lo[j], s_hi[pair, j], s_lo[pair, j])
        for half, slot in enumerate(pairs[pair]):
            acc[slot] -= term[:, half * 128:half * 128 + 128]

    def hops(hop):
        for j in (0, 1, 3, 2):
            arrive(0, hop, j)
            arrive(1, hop, j)

    hops(1)
    chunk_in(3, 0)
    own = jnp.concatenate([g[z, 0, prod], g[z, 1, prod]], axis=0)
    sv_v[...] = jnp.where(c == 0, own[:, :64], own[:, 64:])
    store_s = pltpu.make_async_copy(sv_v, solved_ref, loc_sem.at[3])
    store_s.start()
    for copy in loads:
        copy.wait()
    factor_in(0)
    hops(2)
    chunk_in(0, 0)
    chunk_in(0, 1)
    multiply(0, 0)
    factor_in(3)
    multiply(3, 0)
    hops(3)
    pump(31)
    for j in range(NX):
        arrive(0 if j < 2 else 1, 4, j)
    chunk_in(1, 0)
    chunk_in(1, 1)
    multiply(0, 1)
    multiply(3, 1)
    factor_in(1)
    multiply(1, 0)
    multiply(1, 1)
    chunk_in(2, 0)
    chunk_in(2, 1)
    for j in (0, 3, 1):
        multiply(j, 2)
    chunk_in(3, 1)
    for j in (0, 3, 1):
        multiply(j, 3)
    factor_in(2)
    stores = []
    for pair in range(4):
        multiply(2, pair)
        for slot in pairs[pair]:
            stores.append(pltpu.make_async_copy(acc.at[slot], out_ref.at[:, columns(slot)], o_sem.at[slot]))
            stores[-1].start()
    for copy in sends:
        copy.wait_send()
    for copy in stores:
        copy.wait()
    store_s.wait()


def local(panel_factor, block_inverse, panel_rhs, trailing_rhs):
    ft = panel_factor.T.reshape(2, 32, 8192)
    dma = pltpu.SemaphoreType.DMA
    any_spec = pl.BlockSpec(memory_space=pl.ANY)
    return pl.pallas_call(
        kernel,
        out_shape=(
            jax.ShapeDtypeStruct((64, 64), F32),
            jax.ShapeDtypeStruct((256, 1024), F32),
        ),
        in_specs=[any_spec] * 4,
        out_specs=(any_spec, any_spec),
        scratch_shapes=[
            pltpu.VMEM((64, 128), F32),
            pltpu.VMEM((128, 1024), F32),
            pltpu.VMEM((8, 256, 128), F32),
            pltpu.VMEM((64, 64), F32),
            pltpu.VMEM((16, 32, 128), F32),
            pltpu.VMEM((16, 32, 128), F32),
            pltpu.VMEM((8, 2, 32, 32, 128), F32),
            pltpu.VMEM((2, 32, 32, 256), F32),
            pltpu.VMEM((4, 256, 512), BF16),
            pltpu.VMEM((4, 256, 512), BF16),
            pltpu.VMEM((4, 4, 512, 256), BF16),
            pltpu.VMEM((4, 4, 512, 256), BF16),
            dma((4,)),
            dma((8,)),
            dma((8,)),
            dma((16,)),
            dma((16,)),
            dma((32,)),
            dma((32,)),
            dma((8,)),
            dma((8,)),
            dma((4,)),
            dma((4,)),
            dma((2, 4, 4)),
            dma((2, 4, 4)),
            dma((8, 4)),
            dma((8, 4)),
        ],
        compiler_params=pltpu.CompilerParams(
            collective_id=0, has_side_effects=True, vmem_limit_bytes=60 * 1024 * 1024
        ),
        name="panel_step",
    )(ft, block_inverse, panel_rhs, trailing_rhs)


def solution(mesh):
    in_specs = (P("reg", "prod"), P("prod", "reg"), P("reg", None), P(("reg", "prod"), None))
    out_specs = (P("prod", "reg"), P(("reg", "prod"), None))
    return jax.shard_map(local, mesh=mesh, in_specs=in_specs, out_specs=out_specs, check_vma=False)
```

time: 128 us -> 86.1 us (0.67)
  Pallas kernels: 119 us -> 80.5 us
  local copies, waits for them, and re-layouts: 6.19 us -> 3.68 us
    pallas_call x1, Pallas kernels: 119 us -> 80.5 us  [local(): pl.pallas_call(kernel, out_shape=(jax.ShapeDtypeStruct((64, 64), F32), ja...]
    unnamed x10 -> x2, local copies, waits for them, and re-layouts: 6.19 us -> 3.68 us
where the time goes in v2:
time: 86.1 us; the launch traced here: 84.8 us
  Pallas kernels  80.5 us (93%)
  local copies, waits for them, and re-layouts  3.68 us (4%)
    pallas_call x1, Pallas kernels, local(): pl.pallas_call(kernel, out_shape=(jax.ShapeDtypeStruct((64, 64), F32), ja...  80.5 us
    unnamed x2, local copies, waits for them, and re-layouts  3.68 us

profile of v2, /device:TPU:1, one launch (start us, length us, event | category | flops | bytes accessed | tf_op | source)
XLA Modules:
  0.0 84.8 jit_solution(16698763774183873730)
XLA Ops:
  0.6 80.5 %panel_step.1 = (f32[64,64]{1,0:T(8,128)}, f32[256,1024]{1,0:T(8,128)}) custom-call(f32[2,32,8192]{2,1,0:T(8,128)} %bitcast.3, f32[64,128]{1,0:T(8,128)} %b_ref.1, f32[128,1024]{1,0:T(8,128)} %p_ref.1, f32[256,1024]{1,0:T(8,128)} %t_ref.1), custom_call_target="tpu_custom_call" | custom-call | tf_op jit(solution)/shard_map/panel_step/pallas_call | solution.py:247
  81.1 1.4 %copy.8 = f32[64,64]{1,0:T(8,128)} copy(f32[64,64]{1,0:T(8,128)} %get-tuple-element.4) | data formatting | bytes 32768
  82.5 2.3 %copy.9 = f32[256,1024]{1,0:T(8,128)} copy(f32[256,1024]{1,0:T(8,128)} %get-tuple-element.5) | data formatting | bytes 2097152

commit v3 on v2

--- a/solution.py
+++ b/solution.py
@@ -210,19 +210,21 @@
     multiply(3, 0)
     hops(3)
     pump(31)
-    for j in range(NX):
-        arrive(0 if j < 2 else 1, 4, j)
     chunk_in(1, 0)
     chunk_in(1, 1)
     multiply(0, 1)
     multiply(3, 1)
-    factor_in(1)
-    multiply(1, 0)
-    multiply(1, 1)
+    arrive(0, 4, 0)
+    arrive(1, 4, 3)
     chunk_in(2, 0)
     chunk_in(2, 1)
-    for j in (0, 3, 1):
-        multiply(j, 2)
+    multiply(0, 2)
+    multiply(3, 2)
+    arrive(0, 4, 1)
+    arrive(1, 4, 2)
+    factor_in(1)
+    for pair in range(3):
+        multiply(1, pair)
     chunk_in(3, 1)
     for j in (0, 3, 1):
         multiply(j, 3)

time: 86.1 us -> 85 us (0.987); the launches traced: 84.8 us -> 84.8 us
  no operation moved by 1% of the time
where the time goes in v3:
time: 85 us; the launch traced here: 84.8 us
  Pallas kernels  80.5 us (95%)
  local copies, waits for them, and re-layouts  3.68 us (4%)
    pallas_call x1, Pallas kernels, local(): pl.pallas_call(kernel, out_shape=(jax.ShapeDtypeStruct((64, 64), F32), ja...  80.5 us
    unnamed x2, local copies, waits for them, and re-layouts  3.68 us

profile of v3, /device:TPU:1, one launch (start us, length us, event | category | flops | bytes accessed | tf_op | source)
XLA Modules:
  0.0 84.8 jit_solution(6238755144775787772)
XLA Ops:
  0.6 80.5 %panel_step.1 = (f32[64,64]{1,0:T(8,128)}, f32[256,1024]{1,0:T(8,128)}) custom-call(f32[2,32,8192]{2,1,0:T(8,128)} %bitcast.3, f32[64,128]{1,0:T(8,128)} %b_ref.1, f32[128,1024]{1,0:T(8,128)} %p_ref.1, f32[256,1024]{1,0:T(8,128)} %t_ref.1), custom_call_target="tpu_custom_call" | custom-call | tf_op jit(solution)/shard_map/panel_step/pallas_call | solution.py:249
  81.1 1.4 %copy.8 = f32[64,64]{1,0:T(8,128)} copy(f32[64,64]{1,0:T(8,128)} %get-tuple-element.4) | data formatting | bytes 32768
  82.5 2.3 %copy.9 = f32[256,1024]{1,0:T(8,128)} copy(f32[256,1024]{1,0:T(8,128)} %get-tuple-element.5) | data formatting | bytes 2097152

commit v4 on v2

--- a/solution.py
+++ b/solution.py
@@ -23,13 +23,13 @@
     return acc + jnp.dot(a_hi, b_hi, preferred_element_type=F32)
 
 
-FIRST, SECOND, EACH = 4, 0, 1
+FIRST, SECOND, EACH = 4, 3, 1
 
 
 def kernel(
     ft_ref, b_ref, p_ref, t_ref, solved_ref, out_ref,
-    b_v, p_v, acc, sv_v, part, landed, g, fg, a_hi, a_lo, s_hi, s_lo,
-    loc_sem, t_sem, o_sem, rs_s, rs_r, f_s, f_r, y_s, y_r, x_s, x_r, z_s, z_r, c_s, c_r,
+    b_v, p_v, acc, sv_v, part, paired, landed, g, fx, fg, a_hi, a_lo, s_hi, s_lo,
+    loc_sem, t_sem, o_sem, rs_s, rs_r, fx_s, fx_r, f_s, f_r, y_s, y_r, x_s, x_r, z_s, z_r, w_s, w_r, c_s, c_r,
 ):
     reg, prod = lax.axis_index("reg"), lax.axis_index("prod")
     z, c = reg // 2, reg % 2
@@ -51,10 +51,13 @@
     load_p.start()
 
     barrier = pltpu.get_barrier_semaphore()
-    for d in range(1, 2 * NZ):
-        pl.semaphore_signal(barrier, inc=1, device_id=((reg + d) % (2 * NZ), prod), device_id_type=MESH)
-    for d in range(1, NX * NY):
-        pl.semaphore_signal(barrier, inc=1, device_id=(reg, (prod + d) % (NX * NY)), device_id_type=MESH)
+    pl.semaphore_signal(barrier, inc=1, device_id=(sibling, prod), device_id_type=MESH)
+    for d in range(1, NZ):
+        pl.semaphore_signal(barrier, inc=1, device_id=((reg + 2 * d) % (2 * NZ), prod), device_id_type=MESH)
+    for d in range(1, NX):
+        pl.semaphore_signal(barrier, inc=1, device_id=(reg, ((x + d) % NX) * NY + y), device_id_type=MESH)
+    for d in range(1, NY):
+        pl.semaphore_signal(barrier, inc=1, device_id=(reg, x * NY + (y + d) % NY), device_id_type=MESH)
 
     def chunk_of(slot):
         if slot < 4:
@@ -68,9 +71,9 @@
     load_p.wait()
     product = dot3(*split(b_v[...]), *split(p_v[...]))
     for i in range(2 * NZ):
-        part[i] = product[(i % 2) * 32:(i % 2) * 32 + 32, (i // 2) * 128:(i // 2) * 128 + 128]
-
-    pl.semaphore_wait(barrier, 2 * NZ - 1 + NX * NY - 1)
+        part[i % 2, i // 2] = product[(i % 2) * 32:(i % 2) * 32 + 32, (i // 2) * 128:(i // 2) * 128 + 128]
+
+    pl.semaphore_wait(barrier, NZ + NX - 1 + NY - 1)
 
     sends = []
 
@@ -78,39 +81,65 @@
         copy.start()
         sends.append(copy)
 
+    pair = send(part.at[1 - c], paired, rs_s.at[0], rs_r.at[0], sibling, prod)
+    go(pair)
+
+    stage = {}
+    for dx in (1, 3, 2):
+        j = NX - dx
+        to = (x + dx) % NX
+        stage[j] = send(
+            ft_ref.at[:, :, pl.ds(pl.multiple_of(to * 2048, 2048), 2048)],
+            fx.at[j], fx_s.at[j], fx_r.at[j], reg, to * NY + y,
+        )
+    factor, queue = {}, []
+    for j in (0, 3, 1, 2):
+        for dy in (4, 3, 5, 2, 6, 1, 7):
+            to = (y + dy) % NY
+            if j == 0:
+                src = ft_ref.at[:, :, pl.ds(pl.multiple_of((x * NY + to) * 256, 256), 256)]
+            else:
+                src = fx.at[j, :, :, pl.ds(pl.multiple_of(to * 256, 256), 256)]
+            copy = send(
+                src, fg.at[:, ((x + j) % NX) * NY + y], f_s.at[j, dy], f_r.at[j, dy], reg, x * NY + to
+            )
+            queue.append((j, copy))
+            factor.setdefault(j, []).append(copy)
+    landing = set()
+
+    def pump(count):
+        for _ in range(min(count, len(queue))):
+            j, copy = queue.pop(0)
+            if j > 0 and j not in landing:
+                landing.add(j)
+                stage[j].wait_recv()
+                own_rows = fx.at[j, :, :, pl.ds(pl.multiple_of(y * 256, 256), 256)]
+                keep = pltpu.make_async_copy(own_rows, fg.at[:, ((x + j) % NX) * NY + y], f_r.at[j, 0])
+                keep.start()
+                kept[j] = keep
+            go(copy)
+
+    kept = {}
+
+    pair.wait_recv()
+    part[c] += paired[...]
     rs = []
-    for d in range(1, 2 * NZ):
-        to = (reg + d) % (2 * NZ)
-        copy = send(part.at[to], landed.at[reg], rs_s.at[d], rs_r.at[d], to, prod)
+    for d in (4, 3, 5, 2, 6, 1, 7):
+        to = (z + d) % NZ
+        copy = send(part.at[c, to], landed.at[z], rs_s.at[d], rs_r.at[d], to * 2 + c, prod)
         go(copy)
         rs.append(copy)
 
-    factor, queue = {}, []
-    for dx in (0, 1, 3, 2):
-        for dy in (4, 3, 5, 2, 6, 1, 7, 0):
-            if dx == 0 and dy == 0:
-                continue
-            to = ((x + dx) % NX) * NY + (y + dy) % NY
-            i = dx * NY + dy
-            copy = send(
-                ft_ref.at[:, :, pl.ds(pl.multiple_of(to * 256, 256), 256)],
-                fg.at[:, prod], f_s.at[i], f_r.at[i], reg, to,
-            )
-            queue.append(copy)
-            factor.setdefault((NX - dx) % NX, []).append(copy)
-
-    def pump(count):
-        for _ in range(min(count, len(queue))):
-            go(queue.pop(0))
-
     pump(FIRST)
+    go(stage[3])
+    go(stage[1])
     load_f.start()
     loads = []
     for slot in range(NZ):
         loads.append(pltpu.make_async_copy(t_ref.at[:, columns(slot)], acc.at[slot], t_sem.at[slot]))
         loads[-1].start()
 
-    landed[reg] = part[reg]
+    landed[z] = part[c, z]
     for copy in rs:
         copy.wait_recv()
     g[z, c, prod] = jnp.sum(landed[...], axis=0)
@@ -138,27 +167,52 @@
         go(send(u, u, c_s.at[slot, j], c_r.at[slot, j], sibling, prod))
         pump(EACH)
 
-    xs = {}
-    for dx in (1, 3, 2):
-        u = unit(z, c, 0)
-        copy = send(u, u, x_s.at[dx], x_r.at[dx], reg, ((x + dx) % NX) * NY + y)
-        go(copy)
-        xs[(NX - dx) % NX] = copy
-    relay(0, 0, 0, 0)
-    for j in (1, 3, 2):
-        xs[j].wait_recv()
-        relay(0, j, 0, 0)
+    def along_x(slot, steps):
+        u = unit(chunk_of(slot), c, 0)
+        for dx in steps:
+            j = (NX - dx) % NX
+            go(send(u, u, x_s.at[slot, j], x_r.at[slot, j], reg, ((x + dx) % NX) * NY + y))
+
+    def from_x(slot, j):
+        u = unit(chunk_of(slot), c, j)
+        send(u, u, x_s.at[slot, j], x_r.at[slot, j], reg, prod).wait_recv()
 
     def arrive(way, hop, j):
-        slot = 7 if hop == 4 else hop + 3 * way
+        slot = hop + 3 * way
         u = unit(chunk_of(slot), c, j)
         send(u, u, z_s.at[way, hop - 1, j], z_r.at[way, hop - 1, j], reg, prod).wait_recv()
-        onward = hop < 3 or (hop == 3 and (j < 2) == (way == 0))
+        onward = hop == 1 or (hop == 2 and j in (0, 2))
         relay(
             slot, j,
             hop if way == 0 and onward else None,
             hop if way == 1 and onward else None,
         )
+
+    along_x(0, (1, 3, 2))
+    relay(0, 0, 0, 0)
+    from_x(0, 1)
+    relay(0, 1, 0, 0)
+    arrive(0, 1, 0)
+    arrive(1, 1, 0)
+    from_x(0, 3)
+    relay(0, 3, 0, 0)
+    arrive(0, 2, 0)
+    arrive(1, 2, 0)
+    from_x(0, 2)
+    relay(0, 2, 0, 0)
+    go(stage[2])
+    for way in range(2):
+        arrive(way, 3, 0)
+        along_x(3 + 3 * way, (1, 3))
+    u = unit((z + NZ - 3 + 6 * c) % NZ, c, 0)
+    go(send(u, u, w_s.at[0], w_r.at[0], ((z + NZ + 1 - 2 * c) % NZ) * 2 + c, prod))
+    u = unit(chunk_of(7), c, 0)
+    send(u, u, w_s.at[0], w_r.at[0], reg, prod).wait_recv()
+    along_x(7, (1, 3, 2))
+    relay(7, 0, None, None)
+    for j in (1, 3, 2):
+        arrive(0, 1, j)
+        arrive(1, 1, j)
 
     pairs = ((1, 4), (2, 5), (3, 6), (0, 7))
 
@@ -175,6 +229,8 @@
     def factor_in(j):
         if j == 0:
             load_f.wait()
+        else:
+            kept[j].wait()
         for copy in factor[j]:
             copy.wait_recv()
         for cs in range(2):
@@ -188,12 +244,6 @@
         for half, slot in enumerate(pairs[pair]):
             acc[slot] -= term[:, half * 128:half * 128 + 128]
 
-    def hops(hop):
-        for j in (0, 1, 3, 2):
-            arrive(0, hop, j)
-            arrive(1, hop, j)
-
-    hops(1)
     chunk_in(3, 0)
     own = jnp.concatenate([g[z, 0, prod], g[z, 1, prod]], axis=0)
     sv_v[...] = jnp.where(c == 0, own[:, :64], own[:, 64:])
@@ -202,20 +252,24 @@
     for copy in loads:
         copy.wait()
     factor_in(0)
-    hops(2)
+    for j in (1, 3, 2):
+        arrive(0, 2, j)
+        arrive(1, 2, j)
+    pump(31)
     chunk_in(0, 0)
     chunk_in(0, 1)
     multiply(0, 0)
-    factor_in(3)
-    multiply(3, 0)
-    hops(3)
-    pump(31)
-    for j in range(NX):
-        arrive(0 if j < 2 else 1, 4, j)
     chunk_in(1, 0)
     chunk_in(1, 1)
     multiply(0, 1)
+    factor_in(3)
+    multiply(3, 0)
     multiply(3, 1)
+    for slot, j in ((3, 1), (6, 1), (3, 3), (6, 3), (7, 1), (7, 3), (7, 2)):
+        from_x(slot, j)
+        relay(slot, j, None, None)
+    arrive(0, 3, 2)
+    arrive(1, 3, 2)
     factor_in(1)
     multiply(1, 0)
     multiply(1, 1)
@@ -257,9 +311,11 @@
             pltpu.VMEM((128, 1024), F32),
             pltpu.VMEM((8, 256, 128), F32),
             pltpu.VMEM((64, 64), F32),
-            pltpu.VMEM((16, 32, 128), F32),
-            pltpu.VMEM((16, 32, 128), F32),
+            pltpu.VMEM((2, 8, 32, 128), F32),
+            pltpu.VMEM((8, 32, 128), F32),
+            pltpu.VMEM((8, 32, 128), F32),
             pltpu.VMEM((8, 2, 32, 32, 128), F32),
+            pltpu.VMEM((4, 2, 32, 2048), F32),
             pltpu.VMEM((2, 32, 32, 256), F32),
             pltpu.VMEM((4, 256, 512), BF16),
             pltpu.VMEM((4, 256, 512), BF16),
@@ -268,16 +324,20 @@
             dma((4,)),
             dma((8,)),
             dma((8,)),
-            dma((16,)),
-            dma((16,)),
-            dma((32,)),
-            dma((32,)),
             dma((8,)),
             dma((8,)),
             dma((4,)),
             dma((4,)),
-            dma((2, 4, 4)),
-            dma((2, 4, 4)),
+            dma((4, 8)),
+            dma((4, 8)),
+            dma((8,)),
+            dma((8,)),
+            dma((8, 4)),
+            dma((8, 4)),
+            dma((2, 3, 4)),
+            dma((2, 3, 4)),
+            dma((1,)),
+            dma((1,)),
             dma((8, 4)),
             dma((8, 4)),
         ],

time: 86.1 us -> 85.2 us (0.990)
  no operation moved by 1% of the time
where the time goes in v4:
time: 85.2 us; the launch traced here: 84.1 us
  Pallas kernels  79.7 us (94%)
  local copies, waits for them, and re-layouts  3.68 us (4%)
    pallas_call x1, Pallas kernels, local(): pl.pallas_call(kernel, out_shape=(jax.ShapeDtypeStruct((64, 64), F32), ja...  79.7 us
    unnamed x2, local copies, waits for them, and re-layouts  3.68 us

profile of v4, /device:TPU:1, one launch (start us, length us, event | category | flops | bytes accessed | tf_op | source)
XLA Modules:
  0.0 84.1 jit_solution(1454861173165650955)
XLA Ops:
  0.6 79.7 %panel_step.1 = (f32[64,64]{1,0:T(8,128)}, f32[256,1024]{1,0:T(8,128)}) custom-call(f32[2,32,8192]{2,1,0:T(8,128)} %bitcast.3, f32[64,128]{1,0:T(8,128)} %b_ref.1, f32[128,1024]{1,0:T(8,128)} %p_ref.1, f32[256,1024]{1,0:T(8,128)} %t_ref.1), custom_call_target="tpu_custom_call" | custom-call | tf_op jit(solution)/shard_map/panel_step/pallas_call | solution.py:301
  80.4 1.4 %copy.8 = f32[64,64]{1,0:T(8,128)} copy(f32[64,64]{1,0:T(8,128)} %get-tuple-element.4) | data formatting | bytes 32768
  81.8 2.3 %copy.9 = f32[256,1024]{1,0:T(8,128)} copy(f32[256,1024]{1,0:T(8,128)} %get-tuple-element.5) | data formatting | bytes 2097152
